TPU v7x, 512 devices: a whole 4x8x8 slice. The times are simulated.
512 devices in a mesh: wide: 64 (over z, x, core), replica: 8 (over y).
Axes of the slice: x: 4, y: 8, z: 8, core: 2. Of those that a mesh axis runs over, the one named last changes fastest.
Arguments:
- node_features: bfloat16 [8, 65536, 128], P('replica', 'wide'), may hold values from -6 to 6
- weight_matrix: bfloat16 [128, 256], replicated, may hold values from -0.5 to 0.5
- bias_term: float32 [256], replicated, may hold values from -3 to 3
- adjacency_tiles: bfloat16 [8, 512, 12, 128, 128], P('replica', 'wide'), may hold values from -0.15625 to 0.15625
- tile_column: int32 [8, 512, 12], P('replica', 'wide'), may hold values from 0 to 511, as said below
- tile_count: int32 [8, 512], P('replica', 'wide'), may hold values from 1 to 12, as said below
- grad_hidden: bfloat16 [8, 65536, 256], P('replica', 'wide'), may hold values from -6 to 6
Outputs:
- hidden_out: bfloat16 [8, 65536, 256], P('replica', 'wide')
- weight_grad: float32 [128, 256], replicated
- bias_grad: float32 [256], replicated
Inputs may be any that keep to these rules, and one draw needn't show every extreme that they name: `tile_count`: in every mini-batch some block row has all 12 slots valid. tile_column[b, r, k] differs from r by at most 4, and in every mini-batch both r + 4 and r - 4 occur.
All inputs are finite; a program needn't handle non-finite values.
Results may differ from a plain program's by a relative error of at most 0.012.
Values may be sent and summed in bfloat16 or wider, within the bound.
A program may use at most 128 MiB of HBM per device.

v0:
```python
import jax
import jax.numpy as jnp
from jax import lax
from jax.sharding import PartitionSpec as P

TILE = 128
KT = 12
REACH = 4


def extended_2(x, sides, width):
    for axis, dim in sides:
        size, length = (lax.axis_size(axis), x.shape[dim])
        up = [(i, (i + 1) % size) for i in range(size - 1)]
        down = [(j, i) for i, j in up]
        last = lax.slice_in_dim(x, length - width, length, axis=dim)
        initial = lax.slice_in_dim(x, 0, width, axis=dim)
        before = lax.ppermute(last, axis, up)
        after = lax.ppermute(initial, axis, down)
        x = jnp.concatenate([before, x, after], axis=dim)
    return x


def passed_along(x, axis, by):
    length = lax.axis_size(axis)
    pairs = [(i, i + by) for i in range(length) if 0 <= i + by < length]
    return lax.ppermute(x, axis, pairs)


def on_device(
    node_features, weight_matrix, bias_term, adjacency_tiles, tile_column, tile_count, grad_hidden
):
    features = node_features[0]
    tile_values = adjacency_tiles[0]
    columns = tile_column[0]
    counts = tile_count[0]
    row_blocks = tile_values.shape[0]
    node_rows = features.shape[0]
    rim_rows = REACH * TILE
    span = row_blocks + 2 * REACH
    slot_mask = jnp.arange(KT)[None, :] < counts[:, None]
    first_block = lax.axis_index("wide") * row_blocks - REACH
    local_cols = columns - first_block
    projected = jnp.dot(features, weight_matrix, preferred_element_type=jnp.float32).astype(
        jnp.bfloat16
    )
    extended = extended_2(projected, (("wide", 0),), rim_rows)
    hid_width = extended.shape[1]
    picked = extended.reshape(span, TILE, hid_width)[local_cols]
    picked = picked * slot_mask[:, :, None, None].astype(jnp.bfloat16)
    aggregated = jnp.einsum(
        "rkij,rkjh->rih", tile_values, picked, preferred_element_type=jnp.float32
    )
    aggregated = aggregated.reshape(node_rows, hid_width).astype(jnp.bfloat16)
    preact = aggregated.astype(jnp.float32) + bias_term
    hidden = jax.nn.silu(preact).astype(jnp.bfloat16)
    sigmoid_val = jax.nn.sigmoid(preact)
    grad_pre = (
        grad_hidden[0].astype(jnp.float32) * sigmoid_val * (1.0 + preact * (1.0 - sigmoid_val))
    ).astype(jnp.bfloat16)
    contrib = jnp.einsum(
        "rkij,rih->rkjh",
        tile_values,
        grad_pre.reshape(row_blocks, TILE, hid_width),
        preferred_element_type=jnp.float32,
    )
    onehot = (
        (jnp.arange(span)[:, None] == local_cols.reshape(-1)[None, :])
        & slot_mask.reshape(-1)[None, :]
    ).astype(jnp.float32)
    spread = jnp.dot(
        onehot, contrib.reshape(row_blocks * KT, TILE * hid_width), precision=lax.Precision.HIGHEST
    )
    spread = spread.reshape(span * TILE, hid_width)
    grad_bias = jnp.sum(grad_pre.astype(jnp.float32), axis=0)
    lower_rim = spread[:rim_rows]
    upper_rim = spread[rim_rows + node_rows :]
    from_above = passed_along(lower_rim.astype(jnp.bfloat16), "wide", -1).astype(lower_rim.dtype)
    from_below = passed_along(upper_rim.astype(jnp.bfloat16), "wide", 1).astype(upper_rim.dtype)
    grad_proj = spread[rim_rows : rim_rows + node_rows]
    grad_proj = grad_proj.at[:rim_rows].add(from_below)
    grad_proj = grad_proj.at[node_rows - rim_rows :].add(from_above)
    grad_weight = lax.dot_general(
        features.astype(jnp.float32),
        grad_proj,
        (((0,), (0,)), ((), ())),
        precision=lax.Precision.HIGHEST,
    )
    weight_grad, bias_grad = lax.psum((grad_weight, grad_bias), ("wide", "replica"))
    return (hidden[None], weight_grad, bias_grad)


def solution(mesh):
    return jax.shard_map(
        on_device,
        mesh=mesh,
        in_specs=(
            P("replica", "wide", None),
            P(),
            P(),
            P("replica", "wide", None, None, None),
            P("replica", "wide", None),
            P("replica", "wide"),
            P("replica", "wide", None),
        ),
        out_specs=(P("replica", "wide", None), P(), P()),
        check_vma=False,
    )
```

profile of v0, /device:TPU:1, one launch (start us, length us, event | category | flops | bytes accessed | tf_op | source)
XLA Modules:
  0.0 387.8 jit_solution(1713702534972588926)
XLA Ops:
  10.1 4.5 %collective-permute-start = (bf16[512,256]{1,0:T(8,128)(2,1)}, bf16[512,256]{1,0:T(8,128)(2,1)}, u32[]{:S(2)}, u32[]{:S(2)}) collective-permute-start(bf16[512,256]{1,0:T(8,128)(2,1)} %get-tuple-element.37), channel_id=1, source_target_pairs={{0,8},{8,16},{16,24},{24,32},{32,40},{40,48},{48,56},{56,64},{64,7... | collective-permute-start | bytes 786440 | tf_op jit(solution)/shard_map/ppermute | solution.py:18
  14.6 6.3 %collective-permute-start.1 = (bf16[512,256]{1,0:T(8,128)(2,1)S(1)}, bf16[512,256]{1,0:T(8,128)(2,1)}, u32[]{:S(2)}, u32[]{:S(2)}) collective-permute-start(bf16[512,256]{1,0:T(8,128)(2,1)S(1)} %get-tuple-element.38), channel_id=1, source_target_pairs={{8,0},{16,8},{24,16},{32,24},{40,32},{48,40},{56,48},{64,56},{72,6... | collective-permute-start | bytes 786440 | tf_op jit(solution)/shard_map/ppermute | solution.py:19
  22.6 2.2 pad_maximum_fusion
  24.9 7.2 %gather_fusion = bf16[96,128,256]{2,1,0:T(8,128)(2,1)} fusion(bf16[16,128,256]{2,1,0:T(8,128)(2,1)} %bitcast.88, s32[1024]{0:T(1024)S(1)} %pad_clamp_fusion), kind=kCustom, calls=%fused_computation | custom fusion | bytes 12583296 | tf_op jit(solution)/shard_map/gather | solution.py:49
  32.1 4.2 %fusion.15 = f32[8,256,128]{1,2,0:T(8,128)S(1)} fusion(bf16[8,12,128,256]{3,2,1,0:T(8,128)(2,1)} %bitcast.91, bf16[8,12]{1,0:T(8,128)(2,1)S(1)} %get-tuple-element.40, bf16[1,8,12,128,128]{4,3,2,1,0:T(8,128)(2,1)S(1)} %copy-done), kind=kOutput, calls=%fused_computation.9 | convolution fusion | flops 818413568 | bytes 10485952 | tf_op jit(solution)/shard_map/rkij,rkjh->rih/dot_general | solution.py:51
  37.4 6.3 %convolution_bitcast_fusion = f32[8,12,128,256]{2,3,1,0:T(8,128)} fusion(bf16[1,8,12,128,128]{4,3,2,1,0:T(8,128)(2,1)S(1)} %copy-done, f32[8,256,128]{1,2,0:T(8,128)S(1)} %fusion.15, f32[256]{0:T(256)S(1)} %copy-done.5, bf16[8,128,256]{2,1,0:T(8,128)(2,1)S(1)} %bitcast.92), kind=kOutput, calls=%fused_computation.3 | convolution fusion | flops 808189952 | bytes 17302528 | tf_op jit(solution)/shard_map/rkij,rih->rkjh/dot_general | solution.py:61
  43.7 12.6 %copy.13 = f32[8,12,128,256]{3,2,1,0:T(8,128)} copy(f32[8,12,128,256]{2,3,1,0:T(8,128)} %convolution_bitcast_fusion) | data formatting | bytes 25165824 | tf_op jit(solution)/shard_map/rkij,rih->rkjh/dot_general | solution.py:61
  56.3 17.8 %copy.19 = f32[12,8,128,256]{3,1,2,0:T(8,128)} copy(f32[12,8,128,256]{3,2,1,0:T(8,128)} %bitcast.90) | data formatting | bytes 25165824
  74.1 8.0 %fusion.43 = (bf16[16,32768]{1,0:T(8,128)(2,1)S(1)}, f32[16,32768]{1,0:T(8,128)}) fusion(f32[96,32768]{1,0:T(8,128)} %bitcast.89, s32[96]{0:T(128)S(1)} %sub.36, pred[96]{0:T(512)(128)(4,1)S(1)} %lt.45), kind=kOutput, calls=%fused_computation.48 | convolution fusion | flops 604507136 | bytes 15729120 | tf_op jit(solution)/shard_map/dot_general | solution.py:71
  83.1 1.8 convert_element_type.113
  84.9 1.8 convert_element_type.111
  86.7 1.9 collective-permute-start.2
  88.7 3.3 collective-permute-start.3
  92.0 1.8 convert_reduce_fusion
  93.8 2.1 slice.75
  95.9 2.7 slice.74
  98.6 2.3 slice.65
  100.9 2.2 reshape.213
  103.1 2.0 add_dynamic-update-slice_fusion
  105.1 1.9 fusion.28
  107.0 2.9 convolution_bitcast_fusion.1
  109.9 2.3 multiply_convert_fusion
  112.2 106.3 %psum.15 = f32[256]{0:T(256)} all-reduce(f32[256]{0:T(256)S(1)} %convert_reduce_fusion), channel_id=1, replica_groups=mesh['wide'=64,'replica'=8] {'wide','replica'}, use_global_device_ids=true, to_apply=%region_2.3 | all-reduce | flops 256 | bytes 2048 | tf_op jit(solution)/shard_map/psum | solution.py:89
  218.5 160.8 %all-reduce.2.cloned.1.call-done = f32[128,256]{0,1:T(8,128)} async-done(((f32[128,256]{0,1:T(8,128)}), f32[128,256]{0,1:T(8,128)}) %all-reduce.2.cloned.1.call-update) | async-done | bytes 131088 | tf_op jit(solution)/shard_map/psum | solution.py:89
  (28 shorter events, 8.3 us)
Async XLA Ops:
  7.2 24.9 %copy-start = (bf16[1,8,12,128,128]{4,3,2,1,0:T(8,128)(2,1)S(1)}, bf16[1,8,12,128,128]{4,3,2,1,0:T(8,128)(2,1)}, u32[]{:S(2)}) copy-start(bf16[1,8,12,128,128]{4,3,2,1,0:T(8,128)(2,1)} %param.14) | copy-start | bytes 9437188
  7.2 372.1 %all-reduce.2.cloned.1.call-start = ((), (), s32[]{:S(2)}) async-start(), calls=%async_computation | async-start | bytes 262144 | tf_op jit(solution)/shard_map/psum | solution.py:89
  8.6 0.8 copy-start.2
  10.1 12.5 %collective-permute-start = (bf16[512,256]{1,0:T(8,128)(2,1)}, bf16[512,256]{1,0:T(8,128)(2,1)}, u32[]{:S(2)}, u32[]{:S(2)}) collective-permute-start(bf16[512,256]{1,0:T(8,128)(2,1)} %get-tuple-element.37), channel_id=1, source_target_pairs={{0,8},{8,16},{16,24},{24,32},{32,40},{40,48},{48,56},{56,64},{64,7... | collective-permute-start | bytes 786440 | tf_op jit(solution)/shard_map/ppermute | solution.py:18
  14.6 8.0 %collective-permute-start.1 = (bf16[512,256]{1,0:T(8,128)(2,1)S(1)}, bf16[512,256]{1,0:T(8,128)(2,1)}, u32[]{:S(2)}, u32[]{:S(2)}) collective-permute-start(bf16[512,256]{1,0:T(8,128)(2,1)S(1)} %get-tuple-element.38), channel_id=1, source_target_pairs={{8,0},{16,8},{24,16},{32,24},{40,32},{48,40},{56,48},{64,56},{72,6... | collective-permute-start | bytes 786440 | tf_op jit(solution)/shard_map/ppermute | solution.py:19
  32.1 5.3 %copy-start.3 = (bf16[1,1024,256]{2,1,0:T(8,128)(2,1)S(1)}, bf16[1,1024,256]{2,1,0:T(8,128)(2,1)}, u32[]{:S(2)}) copy-start(bf16[1,1024,256]{2,1,0:T(8,128)(2,1)} %param.17) | copy-start | bytes 1572868
  32.1 5.3 %copy-start.5 = (f32[256]{0:T(256)S(1)}, f32[256]{0:T(256)}, u32[]{:S(2)}) copy-start(f32[256]{0:T(256)} %param.13) | copy-start | bytes 3076
  36.3 1.1 copy-start.1
  82.1 24.9 %copy-start.4 = (bf16[1,1024,128]{2,1,0:T(8,128)(2,1)S(1)}, bf16[1,1024,128]{2,1,0:T(8,128)(2,1)}, u32[]{:S(2)}) copy-start(bf16[1,1024,128]{2,1,0:T(8,128)(2,1)} %param.11) | copy-start | bytes 786436
  86.7 16.4 %collective-permute-start.2 = (bf16[512,256]{1,0:T(8,128)(2,1)}, bf16[512,256]{1,0:T(8,128)(2,1)}, u32[]{:S(2)}, u32[]{:S(2)}) collective-permute-start(bf16[512,256]{1,0:T(8,128)(2,1)} %convert_element_type.111), channel_id=1, source_target_pairs={{0,8},{8,16},{16,24},{24,32},{32,40},{40,48},{48,56},{56,64},{64,7... | collective-permute-start | bytes 786440 | tf_op jit(solution)/shard_map/ppermute | solution.py:27
  88.7 16.4 %collective-permute-start.3 = (bf16[512,256]{1,0:T(8,128)(2,1)}, bf16[512,256]{1,0:T(8,128)(2,1)}, u32[]{:S(2)}, u32[]{:S(2)}) collective-permute-start(bf16[512,256]{1,0:T(8,128)(2,1)} %convert_element_type.113), channel_id=1, source_target_pairs={{8,0},{16,8},{24,16},{32,24},{40,32},{48,40},{56,48},{64,56},{72,6... | collective-permute-start | bytes 786440 | tf_op jit(solution)/shard_map/ppermute | solution.py:27
Sparse Core Ops, SparseCore 0:
  110.1 269.2 all-reduce.1
where the time goes:
time: 389 us; the launch traced here: 388 us
  waiting for transfers between devices  161 us (41%)
  blocking collectives  106 us (27%)
  local copies, waits for them, and re-layouts  56.1 us (14%)
  matrix products  22.8 us (6%)
  starting transfers between devices  16 us (4%)
  between operations  14.1 us (4%)
  other arithmetic  11.7 us (3%)
    psum x1, waiting for transfers between devices, on_device(): lax.psum((grad_weight, grad_bias), ('wide', 'replica'))  161 us
    psum x1, blocking collectives, on_device(): lax.psum((grad_weight, grad_bias), ('wide', 'replica'))  106 us
    unnamed x14, local copies, waits for them, and re-layouts  21.3 us
    dot_general x1, local copies, waits for them, and re-layouts, on_device(): jnp.einsum('rkij,rih->rkjh', tile_values, grad_pre.reshape(row_blocks, TI...  12.6 us
    dot_general x1, matrix products, on_device(): jnp.dot(onehot, contrib.reshape(row_blocks * KT, TILE * hid_width), preci...  8.01 us
  transfers between devices with their start and end apart: 5, of which 1 were waited for; matrix products, arithmetic and copies ran while one was open for 4% of the time, Pallas kernels for 0%

commit v1 on v0

v1 whole, which is shorter than its diff:
```python
import functools

import jax
import jax.numpy as jnp
from jax import lax
from jax.experimental import pallas as pl
from jax.experimental.pallas import tpu as pltpu
from jax.sharding import PartitionSpec as P

TILE = 128
KT = 12
REACH = 4
XC = 8
MESH = pl.DeviceIdType.MESH
BF16 = jnp.bfloat16
F32 = jnp.float32


def far_first(n):
    return sorted(range(1, n), key=lambda j: -min(j, n - j))


def kernel(
    sizes,
    x_ref, w_hbm, b_hbm, a_ref, col_hbm, cnt_hbm, gh_ref,
    hid_ref, dw_ref, bg_ref,
    w_ref, b_ref, col_ref, cnt_ref,
    ext, a_buf, gh_buf, hid_buf, ax_buf, acc, bacc,
    s1, r1, s2, r2, s3, r3, s4, r4,
    a_sem, in_sem, halo_send, halo_recv, out_sem, send_sem, recv_sem,
):
    n_xc, n_y, n_z = sizes
    rows = a_buf.shape[0]
    nodes = rows * TILE
    hid = gh_buf.shape[1]
    part = ax_buf.shape[1] // n_xc
    wide = lax.axis_index("wide")
    y = lax.axis_index("replica")
    n_wide = n_xc * n_z
    z = wide // n_xc
    xc = wide % n_xc

    def xc_dev(j):
        return {"wide": z * n_xc + j, "replica": y}

    def y_dev(j):
        return {"wide": wide, "replica": j}

    def z_dev(j):
        return {"wide": j * n_xc + xc, "replica": y}

    after = {"wide": (wide + 1) % n_wide, "replica": y}
    before = {"wide": (wide + n_wide - 1) % n_wide, "replica": y}

    barrier = pltpu.get_barrier_semaphore()
    greeted = 0
    for n, me, dev in ((n_y, y, y_dev), (n_z, z, z_dev), (n_xc, xc, xc_dev)):
        for j in far_first(n):
            pl.semaphore_signal(
                barrier, inc=1, device_id=dev((me + j) % n), device_id_type=MESH
            )
            greeted += 1
    for dev in (after, before):
        pl.semaphore_signal(barrier, inc=1, device_id=dev, device_id_type=MESH)
        greeted += 1

    x_copy = pltpu.make_async_copy(x_ref, ext.at[pl.ds(REACH, rows)], in_sem.at[0])
    x_copy.start()

    def a_copy(r):
        return pltpu.make_async_copy(a_ref.at[0, r], a_buf.at[r], a_sem.at[r])

    for r in range(rows):
        a_copy(r).start()
    gh_copy = pltpu.make_async_copy(gh_ref.at[0], gh_buf, in_sem.at[1])
    gh_copy.start()
    small = [
        pltpu.make_async_copy(src, dst, in_sem.at[2 + i])
        for i, (src, dst) in enumerate(
            ((col_hbm, col_ref), (cnt_hbm, cnt_ref), (w_hbm, w_ref), (b_hbm, b_ref))
        )
    ]
    for copy in small:
        copy.start()

    pl.semaphore_wait(barrier, greeted)

    to_after = pltpu.make_async_remote_copy(
        src_ref=x_ref.at[pl.ds(rows - REACH, REACH)],
        dst_ref=ext.at[pl.ds(0, REACH)],
        send_sem=halo_send.at[0],
        recv_sem=halo_recv.at[0],
        device_id=after,
        device_id_type=MESH,
    )
    to_before = pltpu.make_async_remote_copy(
        src_ref=x_ref.at[pl.ds(0, REACH)],
        dst_ref=ext.at[pl.ds(REACH + rows, REACH)],
        send_sem=halo_send.at[1],
        recv_sem=halo_recv.at[1],
        device_id=before,
        device_id_type=MESH,
    )
    to_after.start()
    to_before.start()
    for copy in small:
        copy.wait()
    x_copy.wait()
    gh_copy.wait()
    to_after.wait()
    to_before.wait()

    first = wide * rows - REACH

    def aggregate(r, carry):
        a_copy(r).wait()
        count = cnt_ref[0, r]
        picked = []
        for k in range(KT):
            block = ext[jnp.clip(col_ref[0, r, k] - first, 0, rows + 2 * REACH - 1)]
            keep = jnp.clip(count - k, 0, 1).astype(F32)
            picked.append(block * jnp.full(block.shape, keep, F32).astype(BF16))
        tiles = jnp.concatenate([a_buf[r, k] for k in range(KT)], axis=1)
        total = jnp.dot(tiles, jnp.concatenate(picked, axis=0), preferred_element_type=F32)
        ax_buf[pl.ds(pl.multiple_of(r * TILE, TILE), TILE), :] = total.astype(BF16)
        return carry

    lax.fori_loop(0, rows, aggregate, 0)

    acc[...] = jnp.zeros_like(acc)
    bacc[...] = jnp.zeros_like(bacc)
    step = 2 * TILE

    def gates(i, carry):
        here = pl.ds(pl.multiple_of(i * step, step), step)
        ax = ax_buf[here, :]
        total = jnp.dot(ax, w_ref[...], preferred_element_type=F32).astype(BF16)
        preact = total.astype(F32) + b_ref[...]
        s = 1.0 / (1.0 + jnp.exp(-preact))
        hid_buf[here, :] = (preact * s).astype(BF16)
        grad = (gh_buf[here, :].astype(F32) * s * (1.0 + preact * (1.0 - s))).astype(BF16)
        acc[...] += lax.dot_general(
            ax, grad, (((0,), (0,)), ((), ())), preferred_element_type=F32
        )
        bacc[...] += jnp.sum(grad.astype(F32).reshape(step // 8, 8, hid), axis=0)
        return carry

    lax.fori_loop(0, nodes // step, gates, 0)

    hid_copy = pltpu.make_async_copy(hid_buf, hid_ref.at[0], out_sem)
    hid_copy.start()

    half = hid // 2
    for j in range(n_xc):
        s1[j, 0:part] = acc[j * part : (j + 1) * part, 0:half].astype(BF16)
        s1[j, part : 2 * part] = acc[j * part : (j + 1) * part, half:hid].astype(BF16)
    bias = jnp.sum(bacc[...], axis=0, keepdims=True)
    row = lax.broadcasted_iota(jnp.int32, (16, half), 0)
    bias = jnp.where(
        row == 0,
        jnp.broadcast_to(bias[:, 0:half], (16, half)),
        jnp.where(row == 1, jnp.broadcast_to(bias[:, half:hid], (16, half)), 0.0),
    ).astype(BF16)
    for j in range(n_xc):
        s1[j, 2 * part : 2 * part + 16] = bias

    def exchange(stage, n, me, dev, src, dst):
        for j in far_first(n):
            to = (me + j) % n
            pltpu.make_async_remote_copy(
                src_ref=src(to),
                dst_ref=dst.at[me],
                send_sem=send_sem.at[stage],
                recv_sem=recv_sem.at[stage],
                device_id=dev(to),
                device_id_type=MESH,
            ).start()

    def arrive(stage, n, dst):
        whole = dst.at[pl.ds(0, n - 1)]
        pltpu.make_async_copy(whole, whole, recv_sem.at[stage]).wait()

    def sent(stage, n, dst):
        whole = dst.at[pl.ds(0, n - 1)]
        pltpu.make_async_copy(whole, whole, send_sem.at[stage]).wait()

    def summed(n, dst):
        total = dst[0].astype(F32)
        for j in range(1, n):
            total += dst[j].astype(F32)
        return total

    exchange(0, n_xc, xc, xc_dev, lambda j: s1.at[j], r1)
    r1[xc] = s1[xc]
    arrive(0, n_xc, r1)
    s2[...] = summed(n_xc, r1).astype(BF16)

    exchange(1, n_y, y, y_dev, lambda j: s2, r2)
    r2[y] = s2[...]
    arrive(1, n_y, r2)
    s3[...] = summed(n_y, r2).astype(BF16)

    exchange(2, n_z, z, z_dev, lambda j: s3, r3)
    r3[z] = s3[...]
    arrive(2, n_z, r3)
    total = summed(n_z, r3)
    s4[...] = total[0 : 2 * part].astype(BF16)

    exchange(3, n_xc, xc, xc_dev, lambda j: s4, r4)
    r4[xc] = s4[...]
    bg_ref[:, 0:half] = total[2 * part : 2 * part + 1]
    bg_ref[:, half:hid] = total[2 * part + 1 : 2 * part + 2]
    arrive(3, n_xc, r4)
    for j in range(n_xc):
        dw_ref[j * part : (j + 1) * part, 0:half] = r4[j, 0:part].astype(F32)
        dw_ref[j * part : (j + 1) * part, half:hid] = r4[j, part : 2 * part].astype(F32)

    hid_copy.wait()
    sent(0, n_xc, r1)
    sent(1, n_y, r2)
    sent(2, n_z, r3)
    sent(3, n_xc, r4)


def on_device(sizes, x, w, b, a, col, cnt, gh):
    n_xc, n_y, n_z = sizes
    _, rows, kt, tile, _ = a.shape
    nodes, width = x.shape[1:]
    hid = w.shape[1]
    part = width // n_xc
    share = (2 * part + 16, hid // 2)
    only = (2 * part, hid // 2)
    hbm = pl.BlockSpec(memory_space=pl.ANY)
    vmem = pl.BlockSpec(memory_space=pltpu.VMEM)
    hidden, dw, bg = pl.pallas_call(
        functools.partial(kernel, sizes),
        out_shape=(
            jax.ShapeDtypeStruct(gh.shape, BF16),
            jax.ShapeDtypeStruct((width, hid), F32),
            jax.ShapeDtypeStruct((1, hid), F32),
        ),
        in_specs=[hbm] * 7,
        out_specs=(hbm, vmem, vmem),
        scratch_shapes=[
            pltpu.VMEM(w.shape, BF16),
            pltpu.VMEM((1, hid), F32),
            pltpu.SMEM(col.shape, jnp.int32),
            pltpu.SMEM(cnt.shape, jnp.int32),
            pltpu.VMEM((rows + 2 * REACH, tile, width), BF16),
            pltpu.VMEM((rows, kt, tile, tile), BF16),
            pltpu.VMEM((nodes, hid), BF16),
            pltpu.VMEM((nodes, hid), BF16),
            pltpu.VMEM((nodes, width), BF16),
            pltpu.VMEM((width, hid), F32),
            pltpu.VMEM((8, hid), F32),
            pltpu.VMEM((n_xc,) + share, BF16),
            pltpu.VMEM((n_xc,) + share, BF16),
            pltpu.VMEM(share, BF16),
            pltpu.VMEM((n_y,) + share, BF16),
            pltpu.VMEM(share, BF16),
            pltpu.VMEM((n_z,) + share, BF16),
            pltpu.VMEM(only, BF16),
            pltpu.VMEM((n_xc,) + only, BF16),
            pltpu.SemaphoreType.DMA((rows,)),
            pltpu.SemaphoreType.DMA((6,)),
            pltpu.SemaphoreType.DMA((2,)),
            pltpu.SemaphoreType.DMA((2,)),
            pltpu.SemaphoreType.DMA,
            pltpu.SemaphoreType.DMA((4,)),
            pltpu.SemaphoreType.DMA((4,)),
        ],
        compiler_params=pltpu.CompilerParams(
            collective_id=0, has_side_effects=True, vmem_limit_bytes=60 * 2**20
        ),
        cost_estimate=pl.CostEstimate(
            flops=2 * rows * kt * tile * tile * width + 4 * nodes * width * hid,
            bytes_accessed=a.size * 2 + x.size * 2 + gh.size * 4,
            transcendentals=nodes * hid,
        ),
        name="graph_layer",
    )(x.reshape(rows, tile, width), w, b.reshape(1, hid), a, col, cnt, gh)
    return hidden, dw, bg.reshape(hid)


def solution(mesh):
    n_wide, n_y = mesh.shape["wide"], mesh.shape["replica"]
    n_xc = min(XC, n_wide // 2)
    return jax.shard_map(
        functools.partial(on_device, (n_xc, n_y, n_wide // n_xc)),
        mesh=mesh,
        in_specs=(
            P("replica", "wide", None),
            P(),
            P(),
            P("replica", "wide", None, None, None),
            P("replica", "wide", None),
            P("replica", "wide"),
            P("replica", "wide", None),
        ),
        out_specs=(P("replica", "wide", None), P(), P()),
        check_vma=False,
    )
```

time: 389 us -> 48.3 us (0.12)
  waiting for transfers between devices: 161 us -> 0 us
  blocking collectives: 106 us -> 0 us
  local copies, waits for them, and re-layouts: 56.1 us -> 4.66 us
  Pallas kernels: 0 us -> 42.9 us
  matrix products: 22.8 us -> 0 us
  starting transfers between devices: 16 us -> 0 us
  between operations: 14.1 us -> 0.64 us
  other arithmetic: 11.7 us -> 0 us
    psum x1 -> x0, waiting for transfers between devices: 161 us -> none  [on_device(): lax.psum((grad_weight, grad_bias), ('wide', 'replica'))]
    psum x1 -> x0, blocking collectives: 106 us -> none  [on_device(): lax.psum((grad_weight, grad_bias), ('wide', 'replica'))]
    pallas_call x0 -> x1, Pallas kernels: none -> 42.9 us  [on_device(): pl.pallas_call(functools.partial(kernel, sizes), out_shape=(jax.ShapeDtyp...]
    dot_general x5 -> x0, matrix products: 22.8 us -> none  [the longest x1 8.01 us: on_device(): jnp.dot(onehot, contrib.reshape(row_blocks * KT, TILE * hid_width), preci...]
    unnamed x14 -> x3, local copies, waits for them, and re-layouts: 21.3 us -> 4.66 us
    ppermute x4 -> x0, starting transfers between devices: 16 us -> none  [the longest x1 6.27 us: extended_2(): after = lax.ppermute(initial, axis, down)]
    dot_general x1 -> x0, local copies, waits for them, and re-layouts: 12.6 us -> none  [on_device(): jnp.einsum('rkij,rih->rkjh', tile_values, grad_pre.reshape(row_blocks, TI...]
    gather x1 -> x0, local copies, waits for them, and re-layouts: 7.23 us -> none  [on_device(): picked = extended.reshape(span, TILE, hid_width)[local_cols]]
  transfers between devices with their start and end apart: 5 -> 0, of which waited for: 1 -> 0; matrix products, arithmetic and copies ran while one was open for 4% -> 0% of each run, Pallas kernels for 0% -> 0%
where the time goes in v1:
time: 48.3 us; the launch traced here: 48.1 us
  Pallas kernels  42.9 us (89%)
  local copies, waits for them, and re-layouts  4.66 us (10%)
  between operations  0.64 us (1%)
    pallas_call x1, Pallas kernels, on_device(): pl.pallas_call(functools.partial(kernel, sizes), out_shape=(jax.ShapeDtyp...  42.9 us
    unnamed x3, local copies, waits for them, and re-layouts  4.66 us

profile of v1, /device:TPU:1, one launch (start us, length us, event | category | flops | bytes accessed | tf_op | source)
XLA Modules:
  0.0 48.1 jit_solution(554652427381998164)
XLA Ops:
  0.6 42.9 %graph_layer.1 = (bf16[1,1024,256]{2,1,0:T(8,128)(2,1)}, f32[128,256]{1,0:T(8,128)}, f32[1,256]{1,0:T(1,128)}) custom-call(bf16[8,128,128]{2,1,0:T(8,128)(2,1)} %bitcast.3, bf16[128,256]{1,0:T(8,128)(2,1)} %w_hbm.1, f32[1,256]{1,0:T(1,128)} %bitcast.5, bf16[1,8,12,128,128]{4,3,2,1,0:T(8,128)(2,1)} %a_ref.1, s32[1,8,12]{2,1,0:T(8,128)} %col_hbm.1, ...), custom_call_target="tpu_custom_call" | custom-call | flops 536870912 | bytes 4456448 | tf_op jit(solution)/shard_map/graph_layer/pallas_call | solution.py:235
  43.5 1.9 %copy.13 = bf16[1,1024,256]{2,1,0:T(8,128)(2,1)} copy(bf16[1,1024,256]{2,1,0:T(8,128)(2,1)} %get-tuple-element.12) | data formatting | bytes 1048576
  45.4 1.6 %copy.14 = f32[128,256]{1,0:T(8,128)} copy(f32[128,256]{1,0:T(8,128)} %get-tuple-element.13) | data formatting | bytes 262144
  46.9 1.2 %copy.15 = f32[256]{0:T(256)} copy(f32[256]{0:T(256)} %bitcast.4) | data formatting | bytes 2048

commit v2 on v1

--- a/solution.py
+++ b/solution.py
@@ -25,9 +25,10 @@
     x_ref, w_hbm, b_hbm, a_ref, col_hbm, cnt_hbm, gh_ref,
     hid_ref, dw_ref, bg_ref,
     w_ref, b_ref, col_ref, cnt_ref,
-    ext, a_buf, gh_buf, hid_buf, ax_buf, acc, bacc,
+    ext, a_buf, gh_buf, ax_buf,
     s1, r1, s2, r2, s3, r3, s4, r4,
-    a_sem, in_sem, halo_send, halo_recv, out_sem, send_sem, recv_sem,
+    t1, q1, t2, q2, t3, q3,
+    a_sem, in_sem, halo_send, halo_recv, send_sem, recv_sem,
 ):
     n_xc, n_y, n_z = sizes
     rows = a_buf.shape[0]
@@ -54,15 +55,15 @@
 
     barrier = pltpu.get_barrier_semaphore()
     greeted = 0
+    for dev in (after, before):
+        pl.semaphore_signal(barrier, inc=1, device_id=dev, device_id_type=MESH)
+        greeted += 1
     for n, me, dev in ((n_y, y, y_dev), (n_z, z, z_dev), (n_xc, xc, xc_dev)):
         for j in far_first(n):
             pl.semaphore_signal(
                 barrier, inc=1, device_id=dev((me + j) % n), device_id_type=MESH
             )
             greeted += 1
-    for dev in (after, before):
-        pl.semaphore_signal(barrier, inc=1, device_id=dev, device_id_type=MESH)
-        greeted += 1
 
     x_copy = pltpu.make_async_copy(x_ref, ext.at[pl.ds(REACH, rows)], in_sem.at[0])
     x_copy.start()
@@ -112,57 +113,34 @@
 
     first = wide * rows - REACH
 
-    def aggregate(r, carry):
+    for r in range(rows):
         a_copy(r).wait()
         count = cnt_ref[0, r]
         picked = []
         for k in range(KT):
             block = ext[jnp.clip(col_ref[0, r, k] - first, 0, rows + 2 * REACH - 1)]
             keep = jnp.clip(count - k, 0, 1).astype(F32)
-            picked.append(block * jnp.full(block.shape, keep, F32).astype(BF16))
+            picked.append(block * jnp.full((1, block.shape[1]), keep, F32).astype(BF16))
         tiles = jnp.concatenate([a_buf[r, k] for k in range(KT)], axis=1)
         total = jnp.dot(tiles, jnp.concatenate(picked, axis=0), preferred_element_type=F32)
-        ax_buf[pl.ds(pl.multiple_of(r * TILE, TILE), TILE), :] = total.astype(BF16)
-        return carry
-
-    lax.fori_loop(0, rows, aggregate, 0)
-
-    acc[...] = jnp.zeros_like(acc)
-    bacc[...] = jnp.zeros_like(bacc)
-    step = 2 * TILE
-
-    def gates(i, carry):
-        here = pl.ds(pl.multiple_of(i * step, step), step)
-        ax = ax_buf[here, :]
-        total = jnp.dot(ax, w_ref[...], preferred_element_type=F32).astype(BF16)
-        preact = total.astype(F32) + b_ref[...]
-        s = 1.0 / (1.0 + jnp.exp(-preact))
-        hid_buf[here, :] = (preact * s).astype(BF16)
-        grad = (gh_buf[here, :].astype(F32) * s * (1.0 + preact * (1.0 - s))).astype(BF16)
-        acc[...] += lax.dot_general(
-            ax, grad, (((0,), (0,)), ((), ())), preferred_element_type=F32
-        )
-        bacc[...] += jnp.sum(grad.astype(F32).reshape(step // 8, 8, hid), axis=0)
-        return carry
-
-    lax.fori_loop(0, nodes // step, gates, 0)
-
-    hid_copy = pltpu.make_async_copy(hid_buf, hid_ref.at[0], out_sem)
-    hid_copy.start()
+        ax_buf[r * TILE : (r + 1) * TILE, :] = total.astype(BF16)
+
+    ax = ax_buf[...]
+    total = jnp.dot(ax, w_ref[...], preferred_element_type=F32).astype(BF16)
+    preact = total.astype(F32) + b_ref[...]
+    s = 1.0 / (1.0 + jnp.exp(-preact))
+    hid_ref[0] = (preact * s).astype(BF16)
+    grad = (gh_buf[...].astype(F32) * s * (1.0 + preact * (1.0 - s))).astype(BF16)
+    weight = lax.dot_general(
+        ax, grad, (((0,), (0,)), ((), ())), preferred_element_type=F32
+    ).astype(BF16)
+    bias = jnp.sum(grad.astype(F32).reshape(nodes // 8, 8, hid), axis=0)
 
     half = hid // 2
     for j in range(n_xc):
-        s1[j, 0:part] = acc[j * part : (j + 1) * part, 0:half].astype(BF16)
-        s1[j, part : 2 * part] = acc[j * part : (j + 1) * part, half:hid].astype(BF16)
-    bias = jnp.sum(bacc[...], axis=0, keepdims=True)
-    row = lax.broadcasted_iota(jnp.int32, (16, half), 0)
-    bias = jnp.where(
-        row == 0,
-        jnp.broadcast_to(bias[:, 0:half], (16, half)),
-        jnp.where(row == 1, jnp.broadcast_to(bias[:, half:hid], (16, half)), 0.0),
-    ).astype(BF16)
-    for j in range(n_xc):
-        s1[j, 2 * part : 2 * part + 16] = bias
+        s1[j, 0:part] = weight[j * part : (j + 1) * part, 0:half]
+        s1[j, part : 2 * part] = weight[j * part : (j + 1) * part, half:hid]
+    t1[...] = jnp.sum(bias, axis=0, keepdims=True)
 
     def exchange(stage, n, me, dev, src, dst):
         for j in far_first(n):
@@ -192,34 +170,53 @@
 
     exchange(0, n_xc, xc, xc_dev, lambda j: s1.at[j], r1)
     r1[xc] = s1[xc]
+    exchange(4, n_xc, xc, xc_dev, lambda j: t1, q1)
+    q1[xc] = t1[...]
     arrive(0, n_xc, r1)
     s2[...] = summed(n_xc, r1).astype(BF16)
 
     exchange(1, n_y, y, y_dev, lambda j: s2, r2)
     r2[y] = s2[...]
+    arrive(4, n_xc, q1)
+    t2[...] = summed(n_xc, q1)
+    exchange(5, n_y, y, y_dev, lambda j: t2, q2)
+    q2[y] = t2[...]
     arrive(1, n_y, r2)
     s3[...] = summed(n_y, r2).astype(BF16)
 
     exchange(2, n_z, z, z_dev, lambda j: s3, r3)
     r3[z] = s3[...]
+    arrive(5, n_y, q2)
+    t3[...] = summed(n_y, q2)
+    exchange(6, n_z, z, z_dev, lambda j: t3, q3)
+    q3[z] = t3[...]
     arrive(2, n_z, r3)
-    total = summed(n_z, r3)
-    s4[...] = total[0 : 2 * part].astype(BF16)
+    s4[...] = summed(n_z, r3).astype(BF16)
 
     exchange(3, n_xc, xc, xc_dev, lambda j: s4, r4)
     r4[xc] = s4[...]
-    bg_ref[:, 0:half] = total[2 * part : 2 * part + 1]
-    bg_ref[:, half:hid] = total[2 * part + 1 : 2 * part + 2]
+    arrive(6, n_z, q3)
+    bg_ref[...] = summed(n_z, q3)
+    sent(0, n_xc, r1)
+    sent(1, n_y, r2)
+    sent(2, n_z, r3)
+    sent(4, n_xc, q1)
+    sent(5, n_y, q2)
+    sent(6, n_z, q3)
     arrive(3, n_xc, r4)
     for j in range(n_xc):
         dw_ref[j * part : (j + 1) * part, 0:half] = r4[j, 0:part].astype(F32)
         dw_ref[j * part : (j + 1) * part, half:hid] = r4[j, part : 2 * part].astype(F32)
-
-    hid_copy.wait()
-    sent(0, n_xc, r1)
-    sent(1, n_y, r2)
-    sent(2, n_z, r3)
     sent(3, n_xc, r4)
+
+
+def finish(h_in, w_in, b_in, h_out, w_out, b_out, sem):
+    pairs = ((h_in, h_out), (w_in, w_out), (b_in, b_out))
+    copies = [pltpu.make_async_copy(a, b, sem.at[i]) for i, (a, b) in enumerate(pairs)]
+    for copy in copies:
+        copy.start()
+    for copy in copies:
+        copy.wait()
 
 
 def on_device(sizes, x, w, b, a, col, cnt, gh):
@@ -228,19 +225,21 @@
     nodes, width = x.shape[1:]
     hid = w.shape[1]
     part = width // n_xc
-    share = (2 * part + 16, hid // 2)
-    only = (2 * part, hid // 2)
-    hbm = pl.BlockSpec(memory_space=pl.ANY)
+    share = (2 * part, hid // 2)
+    flat = (1, hid)
+    hbm = pl.BlockSpec(memory_space=pltpu.HBM)
+    free = pl.BlockSpec(memory_space=pl.ANY)
     vmem = pl.BlockSpec(memory_space=pltpu.VMEM)
+    operands = (x.reshape(rows, tile, width), w, b.reshape(1, hid), a, col, cnt, gh)
     hidden, dw, bg = pl.pallas_call(
         functools.partial(kernel, sizes),
         out_shape=(
-            jax.ShapeDtypeStruct(gh.shape, BF16),
-            jax.ShapeDtypeStruct((width, hid), F32),
-            jax.ShapeDtypeStruct((1, hid), F32),
+            pltpu.VMEM(gh.shape, BF16),
+            pltpu.VMEM((width, hid), F32),
+            pltpu.VMEM((1, hid), F32),
         ),
         in_specs=[hbm] * 7,
-        out_specs=(hbm, vmem, vmem),
+        out_specs=(vmem,) * 3,
         scratch_shapes=[
             pltpu.VMEM(w.shape, BF16),
             pltpu.VMEM((1, hid), F32),
@@ -249,28 +248,30 @@
             pltpu.VMEM((rows + 2 * REACH, tile, width), BF16),
             pltpu.VMEM((rows, kt, tile, tile), BF16),
             pltpu.VMEM((nodes, hid), BF16),
-            pltpu.VMEM((nodes, hid), BF16),
             pltpu.VMEM((nodes, width), BF16),
-            pltpu.VMEM((width, hid), F32),
-            pltpu.VMEM((8, hid), F32),
             pltpu.VMEM((n_xc,) + share, BF16),
             pltpu.VMEM((n_xc,) + share, BF16),
             pltpu.VMEM(share, BF16),
             pltpu.VMEM((n_y,) + share, BF16),
             pltpu.VMEM(share, BF16),
             pltpu.VMEM((n_z,) + share, BF16),
-            pltpu.VMEM(only, BF16),
-            pltpu.VMEM((n_xc,) + only, BF16),
+            pltpu.VMEM(share, BF16),
+            pltpu.VMEM((n_xc,) + share, BF16),
+            pltpu.VMEM(flat, F32),
+            pltpu.VMEM((n_xc,) + flat, F32),
+            pltpu.VMEM(flat, F32),
+            pltpu.VMEM((n_y,) + flat, F32),
+            pltpu.VMEM(flat, F32),
+            pltpu.VMEM((n_z,) + flat, F32),
             pltpu.SemaphoreType.DMA((rows,)),
             pltpu.SemaphoreType.DMA((6,)),
             pltpu.SemaphoreType.DMA((2,)),
             pltpu.SemaphoreType.DMA((2,)),
-            pltpu.SemaphoreType.DMA,
-            pltpu.SemaphoreType.DMA((4,)),
-            pltpu.SemaphoreType.DMA((4,)),
+            pltpu.SemaphoreType.DMA((7,)),
+            pltpu.SemaphoreType.DMA((7,)),
         ],
         compiler_params=pltpu.CompilerParams(
-            collective_id=0, has_side_effects=True, vmem_limit_bytes=60 * 2**20
+            collective_id=0, has_side_effects=True, vmem_limit_bytes=40 * 2**20
         ),
         cost_estimate=pl.CostEstimate(
             flops=2 * rows * kt * tile * tile * width + 4 * nodes * width * hid,
@@ -278,7 +279,16 @@
             transcendentals=nodes * hid,
         ),
         name="graph_layer",
-    )(x.reshape(rows, tile, width), w, b.reshape(1, hid), a, col, cnt, gh)
+    )(*(pltpu.with_memory_space_constraint(t, pltpu.HBM) for t in operands))
+    hidden, dw, bg = pl.pallas_call(
+        finish,
+        out_shape=tuple(jax.ShapeDtypeStruct(v.shape, v.dtype) for v in (hidden, dw, bg)),
+        in_specs=[free] * 3,
+        out_specs=(hbm,) * 3,
+        scratch_shapes=[pltpu.SemaphoreType.DMA((3,))],
+        compiler_params=pltpu.CompilerParams(vmem_limit_bytes=40 * 2**20),
+        name="finish",
+    )(hidden, dw, bg)
     return hidden, dw, bg.reshape(hid)
 
 

time: 48.3 us -> 42.4 us (0.88)
  local copies, waits for them, and re-layouts: 4.66 us -> 0 us
  Pallas kernels: 42.9 us -> 41.7 us
    unnamed x3 -> x0, local copies, waits for them, and re-layouts: 4.66 us -> none
    pallas_call x1 -> x2, Pallas kernels: 42.9 us -> 41.7 us  [the longest x1 40.8 us: on_device(): pl.pallas_call(functools.partial(kernel, sizes), out_shape=(pltpu.VMEM(gh...]
where the time goes in v2:
time: 42.4 us; the launch traced here: 42.3 us
  Pallas kernels  41.7 us (98%)
  between operations  0.64 us (2%)
    pallas_call x1, Pallas kernels, on_device(): pl.pallas_call(functools.partial(kernel, sizes), out_shape=(pltpu.VMEM(gh...  40.8 us
    pallas_call x1, Pallas kernels, on_device(): pl.pallas_call(finish, out_shape=tuple((jax.ShapeDtypeStruct(v.shape, v.d...  0.86 us

profile of v2, /device:TPU:1, one launch (start us, length us, event | category | flops | bytes accessed | tf_op | source)
XLA Modules:
  0.0 42.3 jit_solution(9468305201786426577)
XLA Ops:
  0.6 40.8 %graph_layer.1 = (bf16[1,1024,256]{2,1,0:T(8,128)(2,1)S(1)}, f32[128,256]{1,0:T(8,128)S(1)}, f32[1,256]{1,0:T(1,128)S(1)}) custom-call(bf16[8,128,128]{2,1,0:T(8,128)(2,1)} %bitcast.3, bf16[128,256]{1,0:T(8,128)(2,1)} %w_hbm.1, f32[1,256]{1,0:T(1,128)} %bitcast.4, bf16[1,8,12,128,128]{4,3,2,1,0:T(8,128)(2,1)} %a_ref.1, s32[1,8,12]{2,1,0:T(8,128)} %col_hbm.1, ...), custom_call_target="tpu_custom_call" | custom-call | flops 536870912 | bytes 4456448 | tf_op jit(solution)/shard_map/graph_layer/pallas_call | solution.py:234
  41.4 0.9 %finish.1 = (bf16[1,1024,256]{2,1,0:T(8,128)(2,1)}, f32[128,256]{1,0:T(8,128)}, f32[1,256]{1,0:T(1,128)}) custom-call(bf16[1,1024,256]{2,1,0:T(8,128)(2,1)S(1)} %get-tuple-element.9.h_in, f32[128,256]{1,0:T(8,128)S(1)} %get-tuple-element.10.w_in, f32[1,256]{1,0:T(1,128)S(1)} %get-tuple-element.11.b_in), custom_call_target="tpu_custom_call" | custom-call | tf_op jit(solution)/shard_map/finish/pallas_call | solution.py:283

commit v3 on v2

--- a/solution.py
+++ b/solution.py
@@ -20,21 +20,26 @@
     return sorted(range(1, n), key=lambda j: -min(j, n - j))
 
 
+def at_distance(n, d):
+    return sorted({d % n, (n - d) % n} - {0})
+
+
 def kernel(
     sizes,
-    x_ref, w_hbm, b_hbm, a_ref, col_hbm, cnt_hbm, gh_ref,
+    x_hbm, w_hbm, b_hbm, a_hbm, col_hbm, cnt_hbm, gh_hbm,
     hid_ref, dw_ref, bg_ref,
     w_ref, b_ref, col_ref, cnt_ref,
-    ext, a_buf, gh_buf, ax_buf,
+    x_ref, halo, a_ref, gh_ref, near, grouped, bacc, acc,
     s1, r1, s2, r2, s3, r3, s4, r4,
     t1, q1, t2, q2, t3, q3,
-    a_sem, in_sem, halo_send, halo_recv, send_sem, recv_sem,
+    a_sem, in_sem, halo_send, halo_recv, send_sem, recv_sem, relay,
 ):
     n_xc, n_y, n_z = sizes
-    rows = a_buf.shape[0]
+    rows = a_ref.shape[0]
     nodes = rows * TILE
-    hid = gh_buf.shape[1]
-    part = ax_buf.shape[1] // n_xc
+    hid = gh_ref.shape[1]
+    width = x_ref.shape[2]
+    part = width // n_xc
     wide = lax.axis_index("wide")
     y = lax.axis_index("replica")
     n_wide = n_xc * n_z
@@ -54,27 +59,24 @@
     before = {"wide": (wide + n_wide - 1) % n_wide, "replica": y}
 
     barrier = pltpu.get_barrier_semaphore()
-    greeted = 0
-    for dev in (after, before):
+
+    def greet(dev):
         pl.semaphore_signal(barrier, inc=1, device_id=dev, device_id_type=MESH)
+
+    rings = ((n_y, y, y_dev), (n_z, z, z_dev))
+    greet(after)
+    greet(before)
+    x_copy = pltpu.make_async_copy(x_hbm, x_ref, in_sem.at[0])
+    x_copy.start()
+    greeted = 2
+    for n, me, dev in rings:
+        for j in at_distance(n, 1):
+            greet(dev((me + j) % n))
+            greeted += 1
+    for j in far_first(n_xc):
+        greet(xc_dev((xc + j) % n_xc))
         greeted += 1
-    for n, me, dev in ((n_y, y, y_dev), (n_z, z, z_dev), (n_xc, xc, xc_dev)):
-        for j in far_first(n):
-            pl.semaphore_signal(
-                barrier, inc=1, device_id=dev((me + j) % n), device_id_type=MESH
-            )
-            greeted += 1
-
-    x_copy = pltpu.make_async_copy(x_ref, ext.at[pl.ds(REACH, rows)], in_sem.at[0])
-    x_copy.start()
-
-    def a_copy(r):
-        return pltpu.make_async_copy(a_ref.at[0, r], a_buf.at[r], a_sem.at[r])
-
-    for r in range(rows):
-        a_copy(r).start()
-    gh_copy = pltpu.make_async_copy(gh_ref.at[0], gh_buf, in_sem.at[1])
-    gh_copy.start()
+
     small = [
         pltpu.make_async_copy(src, dst, in_sem.at[2 + i])
         for i, (src, dst) in enumerate(
@@ -84,57 +86,125 @@
     for copy in small:
         copy.start()
 
+    def a_copy(r):
+        return pltpu.make_async_copy(a_hbm.at[0, r], a_ref.at[r], a_sem.at[r])
+
+    for r in range(rows):
+        a_copy(r).start()
+    gh_copy = pltpu.make_async_copy(gh_hbm.at[0], gh_ref, in_sem.at[1])
+    gh_copy.start()
+
+    x_copy.wait()
     pl.semaphore_wait(barrier, greeted)
 
-    to_after = pltpu.make_async_remote_copy(
-        src_ref=x_ref.at[pl.ds(rows - REACH, REACH)],
-        dst_ref=ext.at[pl.ds(0, REACH)],
-        send_sem=halo_send.at[0],
-        recv_sem=halo_recv.at[0],
-        device_id=after,
-        device_id_type=MESH,
-    )
-    to_before = pltpu.make_async_remote_copy(
-        src_ref=x_ref.at[pl.ds(0, REACH)],
-        dst_ref=ext.at[pl.ds(REACH + rows, REACH)],
-        send_sem=halo_send.at[1],
-        recv_sem=halo_recv.at[1],
-        device_id=before,
-        device_id_type=MESH,
-    )
-    to_after.start()
-    to_before.start()
+    def halo_copy(side):
+        start = rows - REACH if side == 0 else 0
+        return pltpu.make_async_remote_copy(
+            src_ref=x_ref.at[pl.ds(start, REACH)],
+            dst_ref=halo.at[side],
+            send_sem=halo_send.at[side],
+            recv_sem=halo_recv.at[side],
+            device_id=after if side == 0 else before,
+            device_id_type=MESH,
+        )
+
+    halo_copy(0).start()
+    halo_copy(1).start()
+
+    def vouch(ring, d):
+        n, me, dev = rings[ring]
+        for j in at_distance(n, d):
+            pl.semaphore_signal(
+                relay.at[ring, d - 1], inc=1, device_id=dev((me + j) % n), device_id_type=MESH
+            )
+
+    def heard(ring, d):
+        count = len(at_distance(rings[ring][0], d))
+        if count:
+            pl.semaphore_wait(relay.at[ring, d - 1], count)
+
+    vouch(0, 1)
+    vouch(1, 1)
     for copy in small:
         copy.wait()
-    x_copy.wait()
-    gh_copy.wait()
-    to_after.wait()
-    to_before.wait()
-
-    first = wide * rows - REACH
-
+    heard(0, 1)
+    heard(1, 1)
+    vouch(0, 2)
+    vouch(1, 2)
+
+    first = wide * rows
     for r in range(rows):
         a_copy(r).wait()
         count = cnt_ref[0, r]
         picked = []
         for k in range(KT):
-            block = ext[jnp.clip(col_ref[0, r, k] - first, 0, rows + 2 * REACH - 1)]
-            keep = jnp.clip(count - k, 0, 1).astype(F32)
-            picked.append(block * jnp.full((1, block.shape[1]), keep, F32).astype(BF16))
-        tiles = jnp.concatenate([a_buf[r, k] for k in range(KT)], axis=1)
-        total = jnp.dot(tiles, jnp.concatenate(picked, axis=0), preferred_element_type=F32)
-        ax_buf[r * TILE : (r + 1) * TILE, :] = total.astype(BF16)
-
-    ax = ax_buf[...]
-    total = jnp.dot(ax, w_ref[...], preferred_element_type=F32).astype(BF16)
-    preact = total.astype(F32) + b_ref[...]
-    s = 1.0 / (1.0 + jnp.exp(-preact))
-    hid_ref[0] = (preact * s).astype(BF16)
-    grad = (gh_buf[...].astype(F32) * s * (1.0 + preact * (1.0 - s))).astype(BF16)
-    weight = lax.dot_general(
-        ax, grad, (((0,), (0,)), ((), ())), preferred_element_type=F32
-    ).astype(BF16)
-    bias = jnp.sum(grad.astype(F32).reshape(nodes // 8, 8, hid), axis=0)
+            col = col_ref[0, r, k] - first
+            inside = jnp.clip(col, 0, rows - 1)
+            own = 1 - jnp.minimum(jnp.abs(col - inside), 1)
+            keep = (jnp.clip(count - k, 0, 1) * own).astype(F32)
+            block = x_ref[inside]
+            picked.append(block * jnp.full((1, width), keep, F32).astype(BF16))
+        tiles = jnp.concatenate([a_ref[r, k] for k in range(KT)], axis=1)
+        near[r] = jnp.dot(tiles, jnp.concatenate(picked, axis=0), preferred_element_type=F32)
+
+    piece = TILE // 4
+    for r in range(rows):
+        count = cnt_ref[0, r]
+        low = r < REACH
+        blocks = range(r, REACH) if low else range(0, r - rows + REACH + 1)
+        base = first - REACH if low else first + rows
+        weights = {}
+        for h in blocks:
+            for k in range(KT):
+                off = jnp.minimum(jnp.abs(col_ref[0, r, k] - base - h), 1)
+                weights[h, k] = (jnp.clip(count - k, 0, 1) * (1 - off)).astype(F32)
+        for q in range(TILE // piece):
+            here = slice(q * piece, (q + 1) * piece)
+            sums = {h: None for h in blocks}
+            for k in range(KT):
+                tile = a_ref[r, k, here, :].astype(F32)
+                for h in blocks:
+                    term = tile * weights[h, k]
+                    sums[h] = term if sums[h] is None else sums[h] + term
+            for h in range(REACH):
+                lanes = slice(h * TILE, (h + 1) * TILE)
+                if h in blocks:
+                    grouped[r, here, lanes] = sums[h].astype(BF16)
+                else:
+                    grouped[r, here, lanes] = jnp.zeros((piece, TILE), BF16)
+
+    gh_copy.wait()
+    some = REACH * TILE
+
+    def half_pass(side):
+        base = side * REACH
+        pltpu.make_async_copy(halo.at[side], halo.at[side], halo_recv.at[side]).wait()
+        blocks = jnp.concatenate([halo[side, h] for h in range(REACH)], axis=0)
+        ax = jnp.concatenate(
+            [
+                near[base + i] + jnp.dot(grouped[base + i], blocks, preferred_element_type=F32)
+                for i in range(REACH)
+            ],
+            axis=0,
+        ).astype(BF16)
+        here = pl.ds(pl.multiple_of(side * some, some), some)
+        total = jnp.dot(ax, w_ref[...], preferred_element_type=F32).astype(BF16)
+        preact = total.astype(F32) + b_ref[...]
+        s = 1.0 / (1.0 + jnp.exp(-preact))
+        hid_ref[0, here, :] = (preact * s).astype(BF16)
+        grad = (gh_ref[here, :].astype(F32) * s * (1.0 + preact * (1.0 - s))).astype(BF16)
+        weight = lax.dot_general(
+            ax, grad, (((0,), (0,)), ((), ())), preferred_element_type=F32
+        )
+        return weight, jnp.sum(grad.astype(F32).reshape(some // 8, 8, hid), axis=0)
+
+    sooner = 1 - wide % 2
+    weight, bias = half_pass(sooner)
+    acc[...] = weight
+    bacc[...] = bias
+    weight, bias = half_pass(1 - sooner)
+    weight = (acc[...] + weight).astype(BF16)
+    bias = bacc[...] + bias
 
     half = hid // 2
     for j in range(n_xc):
@@ -174,6 +244,8 @@
     q1[xc] = t1[...]
     arrive(0, n_xc, r1)
     s2[...] = summed(n_xc, r1).astype(BF16)
+    heard(0, 2)
+    heard(1, 2)
 
     exchange(1, n_y, y, y_dev, lambda j: s2, r2)
     r2[y] = s2[...]
@@ -197,6 +269,8 @@
     r4[xc] = s4[...]
     arrive(6, n_z, q3)
     bg_ref[...] = summed(n_z, q3)
+    halo_copy(0).wait_send()
+    halo_copy(1).wait_send()
     sent(0, n_xc, r1)
     sent(1, n_y, r2)
     sent(2, n_z, r3)
@@ -245,10 +319,14 @@
             pltpu.VMEM((1, hid), F32),
             pltpu.SMEM(col.shape, jnp.int32),
             pltpu.SMEM(cnt.shape, jnp.int32),
-            pltpu.VMEM((rows + 2 * REACH, tile, width), BF16),
+            pltpu.VMEM((rows, tile, width), BF16),
+            pltpu.VMEM((2, REACH, tile, width), BF16),
             pltpu.VMEM((rows, kt, tile, tile), BF16),
             pltpu.VMEM((nodes, hid), BF16),
-            pltpu.VMEM((nodes, width), BF16),
+            pltpu.VMEM((rows, tile, width), F32),
+            pltpu.VMEM((rows, tile, REACH * tile), BF16),
+            pltpu.VMEM((8, hid), F32),
+            pltpu.VMEM((width, hid), F32),
             pltpu.VMEM((n_xc,) + share, BF16),
             pltpu.VMEM((n_xc,) + share, BF16),
             pltpu.VMEM(share, BF16),
@@ -269,6 +347,7 @@
             pltpu.SemaphoreType.DMA((2,)),
             pltpu.SemaphoreType.DMA((7,)),
             pltpu.SemaphoreType.DMA((7,)),
+            pltpu.SemaphoreType.REGULAR((2, 2)),
         ],
         compiler_params=pltpu.CompilerParams(
             collective_id=0, has_side_effects=True, vmem_limit_bytes=40 * 2**20

time: 42.4 us -> 39.1 us (0.922)
  Pallas kernels: 41.7 us -> 38.3 us
    pallas_call x1, Pallas kernels: 40.8 us -> 37.5 us  [on_device(): pl.pallas_call(functools.partial(kernel, sizes), out_shape=(pltpu.VMEM(gh...]
where the time goes in v3:
time: 39.1 us; the launch traced here: 39 us
  Pallas kernels  38.3 us (98%)
  between operations  0.64 us (2%)
    pallas_call x1, Pallas kernels, on_device(): pl.pallas_call(functools.partial(kernel, sizes), out_shape=(pltpu.VMEM(gh...  37.5 us
    pallas_call x1, Pallas kernels, on_device(): pl.pallas_call(finish, out_shape=tuple((jax.ShapeDtypeStruct(v.shape, v.d...  0.86 us

profile of v3, /device:TPU:1, one launch (start us, length us, event | category | flops | bytes accessed | tf_op | source)
XLA Modules:
  0.0 39.0 jit_solution(17655840888999422404)
XLA Ops:
  0.6 37.5 %graph_layer.1 = (bf16[1,1024,256]{2,1,0:T(8,128)(2,1)S(1)}, f32[128,256]{1,0:T(8,128)S(1)}, f32[1,256]{1,0:T(1,128)S(1)}) custom-call(bf16[8,128,128]{2,1,0:T(8,128)(2,1)} %bitcast.3, bf16[128,256]{1,0:T(8,128)(2,1)} %w_hbm.1, f32[1,256]{1,0:T(1,128)} %bitcast.4, bf16[1,8,12,128,128]{4,3,2,1,0:T(8,128)(2,1)} %a_hbm.1, s32[1,8,12]{2,1,0:T(8,128)} %col_hbm.1, ...), custom_call_target="tpu_custom_call" | custom-call | flops 536870912 | bytes 4456448 | tf_op jit(solution)/shard_map/graph_layer/pallas_call | solution.py:308
  38.1 0.9 %finish.1 = (bf16[1,1024,256]{2,1,0:T(8,128)(2,1)}, f32[128,256]{1,0:T(8,128)}, f32[1,256]{1,0:T(1,128)}) custom-call(bf16[1,1024,256]{2,1,0:T(8,128)(2,1)S(1)} %get-tuple-element.9.h_in, f32[128,256]{1,0:T(8,128)S(1)} %get-tuple-element.10.w_in, f32[1,256]{1,0:T(1,128)S(1)} %get-tuple-element.11.b_in), custom_call_target="tpu_custom_call" | custom-call | tf_op jit(solution)/shard_map/finish/pallas_call | solution.py:362
